TPU v7x, 32 devices: a whole 2x2x4 slice. The times are simulated.
32 devices in a mesh: freq: 8 (over z, x), bl: 4 (over y, core).
Axes of the slice: x: 2, y: 2, z: 4, core: 2. Of those that a mesh axis runs over, the one named last changes fastest.
Arguments:
- voltages: bfloat16 [1024, 134144], P(('bl', 'freq')), may hold values from -6 to 6
- fir_taps: float32 [4, 1024], replicated, may hold values from -3 to 3
- antenna_order: int32 [1024], replicated, may hold values from 0 to 1023, each once
- tile_list: int32 [4, 2], replicated, may hold values from 0 to 3
Outputs:
- visibilities: bfloat16 [4, 512, 256, 512], P('bl', 'freq')
All inputs are finite; a program needn't handle non-finite values.
Results may differ from a plain program's by a relative error of at most 0.0074.
Values may be sent and summed in bfloat16 or wider, within the bound.
A program may use at most 128 MiB of HBM per device.

v0:
```python
import math
import jax
import jax.numpy as jnp
from jax import lax
from jax.sharding import PartitionSpec as P

K = 1024
TAPS = 4
PANEL = 256
SAMPLES = 128


def make_table(points, kept):
    product = (
        jnp.arange(points, dtype=jnp.int32)[:, None]
        * jnp.arange(kept, dtype=jnp.int32)[None, :]
        % points
    )
    phase = 2.0 * math.pi / points * product.astype(jnp.float32)
    return jnp.concatenate([jnp.cos(phase), -jnp.sin(phase)], axis=1).astype(jnp.bfloat16)


def arrange(panel):
    width = panel.shape[1]
    return jnp.transpose(panel, (3, 0, 2, 1)).reshape(panel.shape[3], panel.shape[0], 2 * width)


def rotated(panel):
    turned = jnp.stack([-panel[:, :, 1, :], panel[:, :, 0, :]], axis=2)
    return arrange(turned)


def correlate(source, antenna_order, tile):
    row_ids = lax.dynamic_slice_in_dim(antenna_order, tile[0] * PANEL, PANEL)
    col_ids = lax.dynamic_slice_in_dim(antenna_order, tile[1] * PANEL, PANEL)
    row_panel = jnp.take(source, row_ids, axis=0)
    col_panel = jnp.take(source, col_ids, axis=0)
    left = arrange(row_panel)
    right = jnp.concatenate([arrange(col_panel), rotated(col_panel)], axis=1)
    return jnp.einsum("fps,fqs->fpq", left, right, preferred_element_type=jnp.float32)


def per_device(voltages, fir_taps, antenna_order, tile_list):
    local_count = voltages.shape[0]
    frames = voltages.reshape(local_count, SAMPLES + TAPS - 1, K)
    filtered = jnp.zeros((local_count, SAMPLES, K), jnp.float32)
    for tap in range(TAPS):
        filtered = filtered + fir_taps[tap][None, None, :] * frames[
            :, tap : tap + SAMPLES, :
        ].astype(jnp.float32)
    filtered = filtered.astype(jnp.bfloat16)
    table = make_table(K, K // 2)
    spectra = jnp.dot(
        filtered.reshape(local_count * SAMPLES, K), table, preferred_element_type=jnp.float32
    )
    spectra = (
        (spectra * (1.0 / math.sqrt(K)))
        .astype(jnp.bfloat16)
        .reshape(local_count, SAMPLES, 2, K // 2)
    )
    turned = lax.all_to_all(spectra, "freq", split_axis=3, concat_axis=0, tiled=True)
    gathered = lax.all_gather(turned, "bl", axis=0, tiled=True)
    own_tile = tile_list[lax.axis_index("bl")]
    summed = correlate(gathered, antenna_order, own_tile)
    return (summed / SAMPLES).astype(jnp.bfloat16)[None]


def solution(mesh):
    return jax.shard_map(
        per_device,
        mesh=mesh,
        in_specs=(P(("bl", "freq"), None), P(), P(), P()),
        out_specs=P("bl", "freq", None, None),
        check_vma=False,
    )
```

profile of v0, /device:TPU:0, one launch (start us, length us, event | category | flops | bytes accessed | tf_op | source)
XLA Modules:
  0.0 656.6 jit_solution(10840728497448380260)
XLA Ops:
  6.5 0.0 copy-start
  6.5 0.0 all-gather.2.cloned.1.call-start
  6.5 8.5 %negate_convert_fusion = (bf16[1024,512]{1,0:T(8,128)(2,1)S(1)}, bf16[1024,512]{1,0:T(8,128)(2,1)S(1)}) fusion(), kind=kLoop, calls=%fused_computation.23 | loop fusion | flops 8912896 | bytes 2097152 | tf_op jit(solution)/shard_map/convert.1
  15.1 0.0 copy-start.2
  15.1 9.2 %reshape.35 = bf16[32,131,1024]{2,1,0:T(8,128)(2,1)} reshape(bf16[32,134144]{1,0:T(8,128)(2,1)} %param.6) | data formatting | bytes 17170432 | tf_op jit(solution)/shard_map/reshape | solution.py:45
  24.3 0.0 copy-done.2
  24.3 19.3 %add_convert_fusion = bf16[32,128,1024]{2,1,0:T(8,128)(2,1)S(1)} fusion(bf16[32,131,1024]{2,1,0:T(8,128)(2,1)} %reshape.35, f32[1024]{0:T(1024)S(1)} %bitcast.28, f32[1024]{0:T(1024)S(1)} %bitcast.29, f32[1024]{0:T(1024)S(1)} %bitcast.27, f32[1024]{0:T(1024)S(1)} %bitcast.26), kind=kLoop, calls=%fused_computation.9 | loop fusion | flops 50331648 | bytes 41959424 | tf_op jit(solution)/shard_map/convert_element_type | solution.py:51
  43.6 11.0 %multiply_convert_fusion.1 = bf16[4096,1024]{1,0:T(8,128)(2,1)} fusion(bf16[4096,1024]{1,0:T(8,128)(2,1)S(1)} %bitcast.24, bf16[1024,512]{1,0:T(8,128)(2,1)S(1)} %get-tuple-element.20, bf16[1024,512]{1,0:T(8,128)(2,1)S(1)} %get-tuple-element.21), kind=kOutput, calls=%fused_computation.8 | convolution fusion | flops 8602517504 | bytes 18874368 | tf_op jit(solution)/shard_map/dot_general | solution.py:53
  54.6 14.5 %reshape.37 = bf16[32,128,2,512]{3,2,1,0:T(2,128)(2,1)} reshape(bf16[4096,1024]{1,0:T(8,128)(2,1)} %multiply_convert_fusion.1) | data formatting | bytes 16777216 | tf_op jit(solution)/shard_map/reshape | solution.py:59
  69.1 28.1 %copy.15 = bf16[32,128,2,512]{1,2,0,3:T(2,128)(2,1)} copy(bf16[32,128,2,512]{3,2,1,0:T(2,128)(2,1)} %reshape.37) | data formatting | bytes 16777216 | tf_op jit(solution)/shard_map/reshape | solution.py:59
  97.2 190.4 %all_to_all.18 = bf16[32,128,2,512]{1,2,0,3:T(2,128)(2,1)} all-to-all(bf16[32,128,2,512]{1,2,0,3:T(2,128)(2,1)} %copy.15), channel_id=1, replica_groups=mesh['freq'=8,'bl'=4] {'freq'}, dimensions={3} | all-to-all | bytes 16777216 | tf_op jit(solution)/shard_map/all_to_all | solution.py:61
  287.6 16.5 %copy.16 = bf16[32,128,2,512]{1,3,2,0:T(8,128)(2,1)} copy(bf16[32,128,2,512]{1,2,0,3:T(2,128)(2,1)} %all_to_all.18) | data formatting | bytes 16777216 | tf_op jit(solution)/shard_map/all_to_all | solution.py:61
  304.1 9.8 %copy.17 = bf16[8,32,128,2,64]{2,4,3,1,0:T(8,128)(2,1)} copy(bf16[8,32,128,2,64]{2,4,0,3,1:T(8,128)(2,1)} %bitcast.23) | data formatting | bytes 16777216 | tf_op jit(solution)/shard_map/all_to_all | solution.py:61
  313.9 0.0 copy-start.3
  313.9 0.0 all-gather.2.cloned.1.call-update
  313.9 0.0 copy-done
  313.9 0.1 constant_dynamic-slice_fusion
  314.0 0.5 fusion.19
  315.8 0.0 copy-done.3
  315.8 0.1 compare_and_fusion
  315.9 198.8 %all-gather.2.cloned.1.call-done = bf16[1024,128,2,64]{1,3,2,0:T(8,128)(2,1)} async-done(((bf16[256,128,2,64]{1,3,2,0:T(8,128)(2,1)}), bf16[1024,128,2,64]{1,3,2,0:T(8,128)(2,1)}) %all-gather.2.cloned.1.call-update) | async-done | bytes 33554448 | tf_op jit(solution)/shard_map/all_gather | solution.py:62
  514.7 9.1 %gather_fusion.1 = bf16[256,128,2,64]{1,3,2,0:T(8,128)(2,1)} fusion(bf16[1024,128,2,64]{1,3,2,0:T(8,128)(2,1)} %all-gather.2.cloned.1.call-done, s32[1024]{0:T(1024)S(1)} %get-tuple-element.22), kind=kCustom, calls=%fused_computation.1.clone | custom fusion | bytes 16778240 | tf_op jit(solution)/shard_map/jit(_take)/gather | solution.py:37
  523.8 7.4 %broadcast_select_fusion = bf16[256,128,2,64]{1,3,2,0:T(8,128)(2,1)} fusion(bf16[256,128,2,64]{1,3,2,0:T(8,128)(2,1)} %gather_fusion.1, pred[256]{0:T(512)(128)(4,1)S(1)} %get-tuple-element.6), kind=kLoop, calls=%fused_computation.12 | loop fusion | flops 4194304 | bytes 16777472 | tf_op jit(solution)/shard_map/jit(_take)/select_n | solution.py:37
  531.3 7.4 %fusion.22 = bf16[64,256,2,128]{3,0,2,1:T(8,128)(2,1)} fusion(bf16[256,128,2,64]{1,3,2,0:T(8,128)(2,1)} %gather_fusion.1, pred[256]{0:T(512)(128)(4,1)S(1)} %get-tuple-element.6), kind=kLoop, calls=%fused_computation.39 | loop fusion | flops 4194304 | bytes 16777472 | tf_op jit(solution)/shard_map/transpose | solution.py:25
  538.7 9.1 %gather_fusion = bf16[256,128,2,64]{1,3,2,0:T(8,128)(2,1)} fusion(bf16[1024,128,2,64]{1,3,2,0:T(8,128)(2,1)} %all-gather.2.cloned.1.call-done, s32[1024]{0:T(1024)S(1)} %get-tuple-element.23), kind=kCustom, calls=%fused_computation.clone | custom fusion | bytes 16778240 | tf_op jit(solution)/shard_map/jit(_take)/gather | solution.py:36
  547.8 7.6 %select_bitcast_fusion = bf16[64,256,2,128]{3,0,2,1:T(8,128)(2,1)} fusion(bf16[256,128,2,64]{1,3,2,0:T(8,128)(2,1)} %gather_fusion, pred[256]{0:T(512)(128)(4,1)S(1)} %get-tuple-element.16), kind=kLoop, calls=%fused_computation.11 | loop fusion | flops 4194304 | bytes 16777472 | tf_op jit(solution)/shard_map/transpose | solution.py:25
  555.4 12.9 %copy.18 = bf16[64,256,2,128]{1,3,2,0:T(8,128)(2,1)} copy(bf16[64,256,2,128]{3,0,2,1:T(8,128)(2,1)} %select_bitcast_fusion) | data formatting | bytes 16777216 | tf_op jit(solution)/shard_map/transpose | solution.py:25
  568.3 5.2 slice_negate_fusion
  573.6 6.5 maximum_bitcast_fusion
  580.0 13.2 %copy.20 = bf16[64,256,2,128]{3,2,1,0:T(2,128)(2,1)} copy(bf16[64,256,2,128]{3,0,2,1:T(8,128)(2,1)} %maximum_bitcast_fusion) | data formatting | bytes 16777216 | tf_op jit(solution)/shard_map/transpose | solution.py:25
  593.2 14.1 %reshape.40 = bf16[64,256,256]{2,1,0:T(8,128)(2,1)} reshape(bf16[64,256,2,128]{3,2,1,0:T(2,128)(2,1)} %copy.20) | data formatting | bytes 16777216 | tf_op jit(solution)/shard_map/reshape | solution.py:25
  607.3 13.2 %copy.19 = bf16[64,256,2,128]{3,2,1,0:T(2,128)(2,1)} copy(bf16[64,256,2,128]{3,0,2,1:T(8,128)(2,1)} %fusion.22) | data formatting | bytes 16777216 | tf_op jit(solution)/shard_map/transpose | solution.py:25
  620.4 14.1 %reshape.39 = bf16[64,256,256]{2,1,0:T(8,128)(2,1)} reshape(bf16[64,256,2,128]{3,2,1,0:T(2,128)(2,1)} %copy.19) | data formatting | bytes 16777216 | tf_op jit(solution)/shard_map/reshape | solution.py:25
  634.5 0.0 copy-start.1
  634.5 15.2 %fusion = bf16[1,64,256,512]{3,2,1,0:T(8,128)(2,1)} fusion(bf16[64,256,256]{1,2,0:T(8,128)(2,1)} %bitcast.25, bf16[64,256,256]{2,1,0:T(8,128)(2,1)} %reshape.40, bf16[64,256,256]{2,1,0:T(8,128)(2,1)} %reshape.39), kind=kOutput, calls=%fused_computation.3 | convolution fusion | flops 4345298944 | bytes 41943040 | tf_op jit(solution)/shard_map/fps,fqs->fpq/dot_general | solution.py:40
  649.8 0.0 copy-done.1
  (2 shorter events, 0.0 us)
Async XLA Ops:
  6.5 307.4 %copy-start = (s32[4,2]{0,1:T(2,128)S(1)}, s32[4,2]{0,1:T(2,128)}, u32[]{:S(2)}) copy-start(s32[4,2]{0,1:T(2,128)} %param.9) | copy-start | bytes 100
  6.5 508.2 %all-gather.2.cloned.1.call-start = ((), (), s32[]{:S(2)}) async-start(), calls=%async_computation.1 | async-start | bytes 41943040 | tf_op jit(solution)/shard_map/all_gather | solution.py:62
  15.1 9.2 %copy-start.2 = (f32[4,1024]{1,0:T(4,128)S(1)}, f32[4,1024]{1,0:T(4,128)}, u32[]{:S(2)}) copy-start(f32[4,1024]{1,0:T(4,128)} %param.7) | copy-start | bytes 49156
  313.9 1.9 copy-start.3
  634.5 15.2 %copy-start.1 = (s32[4,2]{0,1:T(2,128)S(1)}, s32[4,2]{0,1:T(2,128)}, u32[]{:S(2)}) copy-start(s32[4,2]{0,1:T(2,128)} %param.9) | copy-start | bytes 100
Sparse Core Ops, SparseCore 0:
  314.0 200.6 all-gather.1
where the time goes:
time: 659 us; the launch traced here: 657 us
  waiting for transfers between devices  199 us (30%)
  blocking collectives  190 us (29%)
  local copies, waits for them, and re-layouts  164 us (25%)
  other arithmetic  62.1 us (9%)
  matrix products  26.2 us (4%)
  between operations  14.7 us (2%)
    all_gather x1, waiting for transfers between devices, per_device(): gathered = lax.all_gather(turned, 'bl', axis=0, tiled=True)  199 us
    all_to_all x1, blocking collectives, per_device(): lax.all_to_all(spectra, 'freq', split_axis=3, concat_axis=0, tiled=True)  190 us
    reshape x2, local copies, waits for them, and re-layouts, per_device(): spectra = (spectra * (1.0 / math.sqrt(K))).astype(jnp.bfloat16).reshape(l...  42.6 us
    transpose x3, local copies, waits for them, and re-layouts, arrange(): jnp.transpose(panel, (3, 0, 2, 1))  39.3 us
    reshape x2, local copies, waits for them, and re-layouts, arrange(): jnp.transpose(panel, (3, 0, 2, 1))  28.2 us
    all_to_all x2, local copies, waits for them, and re-layouts, per_device(): lax.all_to_all(spectra, 'freq', split_axis=3, concat_axis=0, tiled=True)  26.3 us
    transpose x3, other arithmetic, arrange(): jnp.transpose(panel, (3, 0, 2, 1))  21.5 us
    convert_element_type x1, other arithmetic, per_device(): filtered = filtered.astype(jnp.bfloat16)  19.3 us
  transfers between devices with their start and end apart: 1, of which 1 were waited for; matrix products, arithmetic and copies ran while one was open for 0% of the time, Pallas kernels for 0%

commit v1 on v0

--- a/solution.py
+++ b/solution.py
@@ -1,3 +1,4 @@
+import functools
 import math
 import jax
 import jax.numpy as jnp
@@ -8,6 +9,33 @@
 TAPS = 4
 PANEL = 256
 SAMPLES = 128
+
+
+def cover_edge(chunk, dim_i, packet):
+    res, near = (chunk.shape[:dim_i], chunk.shape[dim_i + 1 :])
+    return jnp.moveaxis(chunk.reshape(*res, packet, -1, *near), dim_i, 0)
+
+
+def _tell_sides(mat, out_dim):
+    mat = jnp.moveaxis(mat, 0, out_dim)
+    h_now = mat.shape
+    return mat.reshape(*h_now[:out_dim], h_now[out_dim] * h_now[out_dim + 1], *h_now[out_dim + 2 :])
+
+
+def begin_members_all(own_rows, body, v0, lane_axis):
+    x_now = lax.psum(1, lane_axis)
+    block_out = lax.axis_index(lane_axis)
+    prior, z1 = (x_now, block_out)
+    earlier = cover_edge(own_rows, body, prior)
+    in_order = [earlier[z1]]
+    for nth in range(1, prior):
+        tall = earlier[z1 ^ nth]
+        in_order.append(lax.ppermute(tall, lane_axis, [(ii, ii ^ nth) for ii in range(prior)]))
+    earlier = jnp.stack(in_order, axis=0)[z1 ^ jnp.arange(prior)]
+    return _tell_sides(earlier, v0)
+
+
+_cover_state = functools.partial(begin_members_all, body=3, v0=0, lane_axis="freq")
 
 
 def make_table(points, kept):
@@ -58,7 +86,7 @@
         .astype(jnp.bfloat16)
         .reshape(local_count, SAMPLES, 2, K // 2)
     )
-    turned = lax.all_to_all(spectra, "freq", split_axis=3, concat_axis=0, tiled=True)
+    turned = _cover_state(spectra)
     gathered = lax.all_gather(turned, "bl", axis=0, tiled=True)
     own_tile = tile_list[lax.axis_index("bl")]
     summed = correlate(gathered, antenna_order, own_tile)

time: 659 us -> 625 us (0.948)
  blocking collectives: 190 us -> 0 us
  waiting for transfers between devices: 199 us -> 365 us
  local copies, waits for them, and re-layouts: 164 us -> 141 us
  starting transfers between devices: 0.01 us -> 13.5 us
    all_to_all x1 -> x0, blocking collectives: 190 us -> none  [per_device(): lax.all_to_all(spectra, 'freq', split_axis=3, concat_axis=0, tiled=True)]
    ppermute x0 -> x7, waiting for transfers between devices: none -> 125 us  [begin_members_all(): lax.ppermute(tall, lane_axis, [(ii, ii ^ nth) for ii in range(prior)])]
    reshape x2 -> x0, local copies, waits for them, and re-layouts: 42.6 us -> none  [per_device(): spectra = (spectra * (1.0 / math.sqrt(K))).astype(jnp.bfloat16).reshape(l...]
    all_gather x1, waiting for transfers between devices: 199 us -> 240 us  [per_device(): gathered = lax.all_gather(turned, 'bl', axis=0, tiled=True)]
    all_to_all x2 -> x0, local copies, waits for them, and re-layouts: 26.3 us -> none  [per_device(): lax.all_to_all(spectra, 'freq', split_axis=3, concat_axis=0, tiled=True)]
    unnamed x8 -> x16, local copies, waits for them, and re-layouts: 0.02 us -> 17.3 us
    ppermute x0 -> x7, starting transfers between devices: none -> 13.5 us  [begin_members_all(): lax.ppermute(tall, lane_axis, [(ii, ii ^ nth) for ii in range(prior)])]
    convert_element_type x0 -> x1, local copies, waits for them, and re-layouts: none -> 11.5 us  [per_device(): spectra = (spectra * (1.0 / math.sqrt(K))).astype(jnp.bfloat16).reshape(l...]
  transfers between devices with their start and end apart: 1 -> 8, of which waited for: 1 -> 5; matrix products, arithmetic and copies ran while one was open for 0% -> 2% of each run, Pallas kernels for 0% -> 0%
where the time goes in v1:
time: 625 us; the launch traced here: 623 us
  waiting for transfers between devices  365 us (58%)
  local copies, waits for them, and re-layouts  141 us (23%)
  other arithmetic  62.1 us (10%)
  matrix products  26.2 us (4%)
  between operations  14.8 us (2%)
  starting transfers between devices  13.5 us (2%)
    all_gather x1, waiting for transfers between devices, per_device(): gathered = lax.all_gather(turned, 'bl', axis=0, tiled=True)  240 us
    ppermute x7, waiting for transfers between devices, begin_members_all(): lax.ppermute(tall, lane_axis, [(ii, ii ^ nth) for ii in range(prior)])  125 us
    transpose x3, local copies, waits for them, and re-layouts, arrange(): jnp.transpose(panel, (3, 0, 2, 1))  39.2 us
    reshape x2, local copies, waits for them, and re-layouts, arrange(): jnp.transpose(panel, (3, 0, 2, 1))  28.2 us
    transpose x3, other arithmetic, arrange(): jnp.transpose(panel, (3, 0, 2, 1))  21.5 us
    convert_element_type x1, other arithmetic, per_device(): filtered = filtered.astype(jnp.bfloat16)  19.3 us
    unnamed x16, local copies, waits for them, and re-layouts  17.3 us
    dot_general x1, matrix products, correlate(): jnp.einsum('fps,fqs->fpq', left, right, preferred_element_type=jnp.float32)  15.2 us
  transfers between devices with their start and end apart: 8, of which 5 were waited for; matrix products, arithmetic and copies ran while one was open for 2% of the time, Pallas kernels for 0%

profile of v1, /device:TPU:0, one launch (start us, length us, event | category | flops | bytes accessed | tf_op | source)
XLA Modules:
  0.0 623.0 jit_solution(16674856525271084594)
XLA Ops:
  6.5 0.0 copy-start
  6.5 0.0 all-gather.2.cloned.1.call-start
  6.5 8.5 %negate_convert_fusion = (bf16[1024,512]{1,0:T(8,128)(2,1)S(1)}, bf16[1024,512]{1,0:T(8,128)(2,1)S(1)}) fusion(), kind=kLoop, calls=%fused_computation.24 | loop fusion | flops 8912896 | bytes 2097152 | tf_op jit(solution)/shard_map/convert.1
  15.1 0.0 copy-start.2
  15.1 9.2 %reshape.66 = bf16[32,131,1024]{2,1,0:T(8,128)(2,1)} reshape(bf16[32,134144]{1,0:T(8,128)(2,1)} %param.6) | data formatting | bytes 17170432 | tf_op jit(solution)/shard_map/reshape | solution.py:73
  24.4 0.0 copy-done.2
  24.4 19.3 %add_convert_fusion = bf16[32,128,1024]{2,1,0:T(8,128)(2,1)S(1)} fusion(bf16[32,131,1024]{2,1,0:T(8,128)(2,1)} %reshape.66, f32[1024]{0:T(1024)S(1)} %bitcast.77, f32[1024]{0:T(1024)S(1)} %bitcast.78, f32[1024]{0:T(1024)S(1)} %bitcast.76, f32[1024]{0:T(1024)S(1)} %bitcast.75), kind=kLoop, calls=%fused_computation.10 | loop fusion | flops 50331648 | bytes 41959424 | tf_op jit(solution)/shard_map/convert_element_type | solution.py:79
  43.6 11.0 %multiply_convert_fusion.1 = bf16[4096,1024]{1,0:T(8,128)(2,1)} fusion(bf16[4096,1024]{1,0:T(8,128)(2,1)S(1)} %bitcast.66, bf16[1024,512]{1,0:T(8,128)(2,1)S(1)} %get-tuple-element.28, bf16[1024,512]{1,0:T(8,128)(2,1)S(1)} %get-tuple-element.29), kind=kOutput, calls=%fused_computation.9 | convolution fusion | flops 8602517504 | bytes 18874368 | tf_op jit(solution)/shard_map/dot_general | solution.py:81
  54.6 11.5 %copy.29 = bf16[4096,1024]{0,1:T(8,128)(2,1)} copy(bf16[4096,1024]{1,0:T(8,128)(2,1)} %multiply_convert_fusion.1) | data formatting | bytes 16777216 | tf_op jit(solution)/shard_map/convert_element_type | solution.py:86
  66.1 9.6 %copy.43 = bf16[128,8,32,128]{3,2,1,0:T(8,128)(2,1)} copy(bf16[128,8,32,128]{3,1,2,0:T(8,128)(2,1)} %bitcast.65) | data formatting | bytes 16777216
  75.7 5.0 constant_dynamic-slice_fusion.1
  80.8 0.4 copy.58
  81.2 3.0 collective-permute-start
  84.2 0.4 copy.57
  84.6 1.6 collective-permute-start.1
  86.3 0.4 copy.56
  86.7 0.1 collective-permute-start.2
  86.8 0.4 copy.55
  87.2 3.1 collective-permute-start.3
  90.2 0.4 copy.54
  90.6 1.3 collective-permute-start.4
  92.0 0.4 copy.53
  92.4 0.4 copy.52
  92.8 1.4 bitcast_dynamic-update-slice_fusion.7
  94.2 13.2 %collective-permute-done = bf16[32,128,2,64]{1,3,2,0:T(8,128)(2,1)S(1)} collective-permute-done((bf16[32,128,2,64]{1,3,2,0:T(8,128)(2,1)S(1)}, bf16[32,128,2,64]{1,3,2,0:T(8,128)(2,1)S(1)}, u32[]{:S(2)}, u32[]{:S(2)}) %collective-permute-start) | collective-permute-done | bytes 1048608 | tf_op jit(solution)/shard_map/ppermute | solution.py:33
  107.4 3.8 collective-permute-start.5
  111.2 1.0 bitcast_dynamic-update-slice_fusion.6
  112.3 42.0 %collective-permute-done.1 = bf16[32,128,2,64]{1,3,2,0:T(8,128)(2,1)S(1)} collective-permute-done((bf16[32,128,2,64]{1,3,2,0:T(8,128)(2,1)S(1)}, bf16[32,128,2,64]{1,3,2,0:T(8,128)(2,1)S(1)}, u32[]{:S(2)}, u32[]{:S(2)}) %collective-permute-start.1) | collective-permute-done | bytes 1048608 | tf_op jit(solution)/shard_map/ppermute | solution.py:33
  154.3 0.6 collective-permute-start.6
  154.9 1.0 bitcast_dynamic-update-slice_fusion.5
  155.9 18.4 %collective-permute-done.2 = bf16[32,128,2,64]{1,3,2,0:T(8,128)(2,1)S(1)} collective-permute-done((bf16[32,128,2,64]{1,3,2,0:T(8,128)(2,1)S(1)}, bf16[32,128,2,64]{1,3,2,0:T(8,128)(2,1)S(1)}, u32[]{:S(2)}, u32[]{:S(2)}) %collective-permute-start.2) | collective-permute-done | bytes 1048608 | tf_op jit(solution)/shard_map/ppermute | solution.py:33
  174.4 1.0 bitcast_dynamic-update-slice_fusion.4
  175.4 0.0 collective-permute-done.3
  175.4 1.0 bitcast_dynamic-update-slice_fusion.3
  176.5 51.5 %collective-permute-done.4 = bf16[32,128,2,64]{1,3,2,0:T(8,128)(2,1)S(1)} collective-permute-done((bf16[32,128,2,64]{1,3,2,0:T(8,128)(2,1)S(1)}, bf16[32,128,2,64]{1,3,2,0:T(8,128)(2,1)S(1)}, u32[]{:S(2)}, u32[]{:S(2)}) %collective-permute-start.4) | collective-permute-done | bytes 1048608 | tf_op jit(solution)/shard_map/ppermute | solution.py:33
  227.9 1.0 bitcast_dynamic-update-slice_fusion.2
  229.0 0.0 collective-permute-done.5
  229.0 1.0 bitcast_dynamic-update-slice_fusion.1
  230.0 0.0 collective-permute-done.6
  230.0 1.0 bitcast_dynamic-update-slice_fusion
  231.1 8.1 %gather_fusion = bf16[8,32,128,2,64]{2,4,3,1,0:T(8,128)(2,1)} fusion(bf16[8,32,128,2,64]{2,4,3,1,0:T(8,128)(2,1)} %bitcast_dynamic-update-slice_fusion, s32[1024]{0:T(1024)S(1)} %pad_clamp_fusion.2), kind=kCustom, calls=%fused_computation.2 | custom fusion | bytes 16777248 | tf_op jit(solution)/shard_map/gather | solution.py:34
  239.1 0.0 copy-start.3
  239.1 0.0 all-gather.2.cloned.1.call-update
  239.2 0.0 copy-done
  239.2 0.1 constant_dynamic-slice_fusion
  239.2 0.6 fusion.20
  241.1 0.0 copy-done.3
  241.1 0.1 compare_and_fusion
  241.2 239.9 %all-gather.2.cloned.1.call-done = bf16[1024,128,2,64]{1,3,2,0:T(8,128)(2,1)} async-done(((bf16[256,128,2,64]{1,3,2,0:T(8,128)(2,1)}), bf16[1024,128,2,64]{1,3,2,0:T(8,128)(2,1)}) %all-gather.2.cloned.1.call-update) | async-done | bytes 33554448 | tf_op jit(solution)/shard_map/all_gather | solution.py:90
  481.1 9.1 %gather_fusion.2 = bf16[256,128,2,64]{1,3,2,0:T(8,128)(2,1)} fusion(bf16[1024,128,2,64]{1,3,2,0:T(8,128)(2,1)} %all-gather.2.cloned.1.call-done, s32[1024]{0:T(1024)S(1)} %get-tuple-element.30), kind=kCustom, calls=%fused_computation.1.clone | custom fusion | bytes 16778240 | tf_op jit(solution)/shard_map/jit(_take)/gather | solution.py:65
  490.2 7.4 %broadcast_select_fusion = bf16[256,128,2,64]{1,3,2,0:T(8,128)(2,1)} fusion(bf16[256,128,2,64]{1,3,2,0:T(8,128)(2,1)} %gather_fusion.2, pred[256]{0:T(512)(128)(4,1)S(1)} %get-tuple-element.6), kind=kLoop, calls=%fused_computation.13 | loop fusion | flops 4194304 | bytes 16777472 | tf_op jit(solution)/shard_map/jit(_take)/select_n | solution.py:65
  497.6 7.4 %fusion.23 = bf16[64,256,2,128]{3,0,2,1:T(8,128)(2,1)} fusion(bf16[256,128,2,64]{1,3,2,0:T(8,128)(2,1)} %gather_fusion.2, pred[256]{0:T(512)(128)(4,1)S(1)} %get-tuple-element.6), kind=kLoop, calls=%fused_computation.66 | loop fusion | flops 4194304 | bytes 16777472 | tf_op jit(solution)/shard_map/transpose | solution.py:53
  505.1 9.1 %gather_fusion.1 = bf16[256,128,2,64]{1,3,2,0:T(8,128)(2,1)} fusion(bf16[1024,128,2,64]{1,3,2,0:T(8,128)(2,1)} %all-gather.2.cloned.1.call-done, s32[1024]{0:T(1024)S(1)} %get-tuple-element.31), kind=kCustom, calls=%fused_computation.clone | custom fusion | bytes 16778240 | tf_op jit(solution)/shard_map/jit(_take)/gather | solution.py:64
  514.2 7.6 %select_bitcast_fusion = bf16[64,256,2,128]{3,0,2,1:T(8,128)(2,1)} fusion(bf16[256,128,2,64]{1,3,2,0:T(8,128)(2,1)} %gather_fusion.1, pred[256]{0:T(512)(128)(4,1)S(1)} %get-tuple-element.24), kind=kLoop, calls=%fused_computation.12 | loop fusion | flops 4194304 | bytes 16777472 | tf_op jit(solution)/shard_map/transpose | solution.py:53
  521.8 12.9 %copy.38 = bf16[64,256,2,128]{1,3,2,0:T(8,128)(2,1)} copy(bf16[64,256,2,128]{3,0,2,1:T(8,128)(2,1)} %select_bitcast_fusion) | data formatting | bytes 16777216 | tf_op jit(solution)/shard_map/transpose | solution.py:53
  534.7 5.3 slice_negate_fusion
  539.9 6.5 %maximum_bitcast_fusion = bf16[64,256,2,128]{3,0,2,1:T(8,128)(2,1)} fusion(bf16[256,128,1,64]{1,3,2,0:T(8,128)(2,1)} %get-tuple-element.11, bf16[256,128,1,64]{1,3,2,0:T(8,128)(2,1)S(1)} %get-tuple-element.10), kind=kLoop, calls=%fused_computation.11 | loop fusion | flops 4194304 | bytes 16777216 | tf_op jit(solution)/shard_map/transpose | solution.py:53
  546.4 13.2 %copy.40 = bf16[64,256,2,128]{3,2,1,0:T(2,128)(2,1)} copy(bf16[64,256,2,128]{3,0,2,1:T(8,128)(2,1)} %maximum_bitcast_fusion) | data formatting | bytes 16777216 | tf_op jit(solution)/shard_map/transpose | solution.py:53
  559.6 14.1 %reshape.71 = bf16[64,256,256]{2,1,0:T(8,128)(2,1)} reshape(bf16[64,256,2,128]{3,2,1,0:T(2,128)(2,1)} %copy.40) | data formatting | bytes 16777216 | tf_op jit(solution)/shard_map/reshape | solution.py:53
  573.7 13.2 %copy.39 = bf16[64,256,2,128]{3,2,1,0:T(2,128)(2,1)} copy(bf16[64,256,2,128]{3,0,2,1:T(8,128)(2,1)} %fusion.23) | data formatting | bytes 16777216 | tf_op jit(solution)/shard_map/transpose | solution.py:53
  586.9 14.1 %reshape.70 = bf16[64,256,256]{2,1,0:T(8,128)(2,1)} reshape(bf16[64,256,2,128]{3,2,1,0:T(2,128)(2,1)} %copy.39) | data formatting | bytes 16777216 | tf_op jit(solution)/shard_map/reshape | solution.py:53
  600.9 0.0 copy-start.1
  600.9 15.2 %fusion = bf16[1,64,256,512]{3,2,1,0:T(8,128)(2,1)} fusion(bf16[64,256,256]{1,2,0:T(8,128)(2,1)} %bitcast.67, bf16[64,256,256]{2,1,0:T(8,128)(2,1)} %reshape.71, bf16[64,256,256]{2,1,0:T(8,128)(2,1)} %reshape.70), kind=kOutput, calls=%fused_computation.4 | convolution fusion | flops 4345298944 | bytes 41943040 | tf_op jit(solution)/shard_map/fps,fqs->fpq/dot_general | solution.py:68
  616.1 0.0 copy-done.1
  (4 shorter events, 0.0 us)
Async XLA Ops:
  6.5 232.6 %copy-start = (s32[4,2]{0,1:T(2,128)S(1)}, s32[4,2]{0,1:T(2,128)}, u32[]{:S(2)}) copy-start(s32[4,2]{0,1:T(2,128)} %param.9) | copy-start | bytes 100
  6.5 474.6 %all-gather.2.cloned.1.call-start = ((), (), s32[]{:S(2)}) async-start(), calls=%async_computation | async-start | bytes 41943040 | tf_op jit(solution)/shard_map/all_gather | solution.py:90
  15.1 9.2 %copy-start.2 = (f32[4,1024]{1,0:T(4,128)S(1)}, f32[4,1024]{1,0:T(4,128)}, u32[]{:S(2)}) copy-start(f32[4,1024]{1,0:T(4,128)} %param.7) | copy-start | bytes 49156
  81.2 26.2 %collective-permute-start = (bf16[32,128,2,64]{1,3,2,0:T(8,128)(2,1)S(1)}, bf16[32,128,2,64]{1,3,2,0:T(8,128)(2,1)S(1)}, u32[]{:S(2)}, u32[]{:S(2)}) collective-permute-start(bf16[32,128,2,64]{1,3,2,0:T(8,128)(2,1)S(1)} %bitcast.74), channel_id=1, source_target_pairs={{0,4},{4,0},{8,12},{12,8},{16,20},{20,16},{24,28},{28,24},{1,5},{5... | collective-permute-start | bytes 3145736 | tf_op jit(solution)/shard_map/ppermute | solution.py:33
  84.6 69.7 %collective-permute-start.1 = (bf16[32,128,2,64]{1,3,2,0:T(8,128)(2,1)S(1)}, bf16[32,128,2,64]{1,3,2,0:T(8,128)(2,1)S(1)}, u32[]{:S(2)}, u32[]{:S(2)}) collective-permute-start(bf16[32,128,2,64]{1,3,2,0:T(8,128)(2,1)S(1)} %bitcast.73), channel_id=1, source_target_pairs={{0,8},{4,12},{8,0},{12,4},{16,24},{20,28},{24,16},{28,20},{1,9},{5... | collective-permute-start | bytes 3145736 | tf_op jit(solution)/shard_map/ppermute | solution.py:33
  86.7 87.7 %collective-permute-start.2 = (bf16[32,128,2,64]{1,3,2,0:T(8,128)(2,1)S(1)}, bf16[32,128,2,64]{1,3,2,0:T(8,128)(2,1)S(1)}, u32[]{:S(2)}, u32[]{:S(2)}) collective-permute-start(bf16[32,128,2,64]{1,3,2,0:T(8,128)(2,1)S(1)} %bitcast.72), channel_id=1, source_target_pairs={{0,12},{4,8},{8,4},{12,0},{16,28},{20,24},{24,20},{28,16},{1,13},{... | collective-permute-start | bytes 3145736 | tf_op jit(solution)/shard_map/ppermute | solution.py:33
  87.2 88.2 %collective-permute-start.3 = (bf16[32,128,2,64]{1,3,2,0:T(8,128)(2,1)S(1)}, bf16[32,128,2,64]{1,3,2,0:T(8,128)(2,1)S(1)}, u32[]{:S(2)}, u32[]{:S(2)}) collective-permute-start(bf16[32,128,2,64]{1,3,2,0:T(8,128)(2,1)S(1)} %bitcast.71), channel_id=1, source_target_pairs={{0,16},{4,20},{8,24},{12,28},{16,0},{20,4},{24,8},{28,12},{1,17},{... | collective-permute-start | bytes 3145736 | tf_op jit(solution)/shard_map/ppermute | solution.py:33
  90.6 137.3 %collective-permute-start.4 = (bf16[32,128,2,64]{1,3,2,0:T(8,128)(2,1)S(1)}, bf16[32,128,2,64]{1,3,2,0:T(8,128)(2,1)S(1)}, u32[]{:S(2)}, u32[]{:S(2)}) collective-permute-start(bf16[32,128,2,64]{1,3,2,0:T(8,128)(2,1)S(1)} %bitcast.70), channel_id=1, source_target_pairs={{0,20},{4,16},{8,28},{12,24},{16,4},{20,0},{24,12},{28,8},{1,21},{... | collective-permute-start | bytes 3145736 | tf_op jit(solution)/shard_map/ppermute | solution.py:33
  107.4 121.6 %collective-permute-start.5 = (bf16[32,128,2,64]{1,3,2,0:T(8,128)(2,1)S(1)}, bf16[32,128,2,64]{1,3,2,0:T(8,128)(2,1)S(1)}, u32[]{:S(2)}, u32[]{:S(2)}) collective-permute-start(bf16[32,128,2,64]{1,3,2,0:T(8,128)(2,1)S(1)} %bitcast.69), channel_id=1, source_target_pairs={{0,24},{4,28},{8,16},{12,20},{16,8},{20,12},{24,0},{28,4},{1,25},{... | collective-permute-start | bytes 3145736 | tf_op jit(solution)/shard_map/ppermute | solution.py:33
  154.3 75.7 %collective-permute-start.6 = (bf16[32,128,2,64]{1,3,2,0:T(8,128)(2,1)S(1)}, bf16[32,128,2,64]{1,3,2,0:T(8,128)(2,1)S(1)}, u32[]{:S(2)}, u32[]{:S(2)}) collective-permute-start(bf16[32,128,2,64]{1,3,2,0:T(8,128)(2,1)S(1)} %bitcast.68), channel_id=1, source_target_pairs={{0,28},{4,24},{8,20},{12,16},{16,12},{20,8},{24,4},{28,0},{1,29},{... | collective-permute-start | bytes 3145736 | tf_op jit(solution)/shard_map/ppermute | solution.py:33
  239.1 2.0 copy-start.3
  600.9 15.2 %copy-start.1 = (s32[4,2]{0,1:T(2,128)S(1)}, s32[4,2]{0,1:T(2,128)}, u32[]{:S(2)}) copy-start(s32[4,2]{0,1:T(2,128)} %param.9) | copy-start | bytes 100
Sparse Core Ops, SparseCore 0:
  239.3 241.7 all-gather.1
